TPU v7x, 32 devices: a whole 2x2x4 slice. The times are simulated.
32 devices in a mesh: section: 4 (over y, x), tensor: 2 (over core), dp: 4 (over z).
Axes of the slice: x: 2, y: 2, z: 4, core: 2. Of those that a mesh axis runs over, the one named last changes fastest.
Arguments:
- hidden: bfloat16 [4, 64, 8192], P('dp'), may hold values from -6 to 6
- lengths: int32 [4, 4], replicated, may hold values from 1 to 48, 64 in all within a row
- targets: int32 [4, 64], replicated, may hold values from 0 to 65535
- attn_gain: float32 [4, 8192], P('section'), may hold values from 0.25 to 1.75
- w_query: bfloat16 [4, 8192, 4096], P('section', None, ('tensor', 'dp')), as said below
- w_key: bfloat16 [4, 8192, 512], P('section', None, 'tensor'), may hold values from -0.0625 to 0.0625
- w_value: bfloat16 [4, 8192, 512], P('section', None, 'tensor'), may hold values from -0.0625 to 0.0625
- w_out: bfloat16 [4, 4096, 8192], P('section', ('tensor', 'dp')), may hold values from -0.09375 to 0.09375
- final_gain: float32 [8192], replicated, may hold values from 0.25 to 1.75
- unembed: bfloat16 [8192, 65536], P(None, ('section', 'tensor', 'dp')), as said below
Outputs:
- logprob: float32 [4, 64], replicated
Inputs may be any that keep to these rules, and one draw needn't show every extreme that they name: Each row's 4 lengths sum to 64; in every row the longest is exactly 48. `w_query`: real-valued projection weights. `unembed`: real-valued output embedding.
All inputs are finite; a program needn't handle non-finite values.
Results may differ from a plain program's by a relative error of at most 0.018.
The roundings to bfloat16 on the way count: a program that leaves them out, or rounds other values in their place, can miss the bound.
Values may be sent and summed in bfloat16 or wider, within the bound.
A program may use at most 256 MiB of HBM per device.

v0:
```python
import jax
import jax.numpy as jnp
from jax import lax
from jax.sharding import PartitionSpec as P

HEADS = 64
HD = 64
KVH = 8


EPS = 1e-05
ROPE_BASE = 500000.0
NEGATIVE = -1e30


def shifted(value, axis, steps):
    count = lax.axis_size(axis)
    pairs = [(source, (source + steps) % count) for source in range(count)]
    return lax.ppermute(value, axis, pairs)


def from_root(x, axis, root):
    mine = lax.axis_index(axis) == root
    return lax.psum(jnp.where(mine, x, jnp.zeros_like(x)), axis)


def norm_round(block_rows, gain_row):
    widened = block_rows.astype(jnp.float32)
    inverse = lax.rsqrt(jnp.mean(widened * widened, axis=-1, keepdims=True) + EPS)
    return (widened * inverse * gain_row).astype(jnp.bfloat16)


def segments(lengths, length):
    seq_ends = jnp.cumsum(lengths, axis=-1, dtype=jnp.int32)
    places = jnp.arange(length, dtype=jnp.int32)
    passed = seq_ends[:, None, :] <= places[None, :, None]
    owners = jnp.sum(passed.astype(jnp.int32), axis=-1, dtype=jnp.int32)
    offset = jnp.sum(jnp.where(passed, lengths[:, None, :], 0), axis=-1, dtype=jnp.int32)
    return (owners, places[None, :] - offset)


def rotate(values, positions):
    half_dim = values.shape[-1] // 2
    frequency = jnp.power(
        ROPE_BASE, -2.0 * jnp.arange(half_dim, dtype=jnp.float32) / values.shape[-1]
    )
    angles = positions.astype(jnp.float32)[..., None] * frequency
    cosines = jnp.cos(angles)[..., None, :]
    sine_vals = jnp.sin(angles)[..., None, :]
    front_half = values[..., :half_dim]
    back_half = values[..., half_dim:]
    return jnp.concatenate(
        [
            front_half * cosines - back_half * sine_vals,
            back_half * cosines + front_half * sine_vals,
        ],
        axis=-1,
    )


def attend(queries, key_rows, value_rows, key_head, key_owner, query_owner, query_place):
    picked_keys = jnp.take(key_rows, key_head, axis=2)
    picked_values = jnp.take(value_rows, key_head, axis=2)
    scores = jnp.einsum(
        "gphd,gshd->ghps", queries, picked_keys, preferred_element_type=jnp.float32
    ) * queries.shape[-1] ** (-0.5)
    key_place = jnp.arange(key_rows.shape[1], dtype=jnp.int32)
    allowed = (key_owner[:, None, :] == query_owner[:, :, None]) & (
        key_place[None, None, :] <= query_place[None, :, None]
    )
    allowed = allowed[:, None, :, :]
    highest = jnp.max(jnp.where(allowed, scores, NEGATIVE), axis=-1, keepdims=True)
    raised = jnp.where(allowed, jnp.exp(scores - highest), 0.0)
    weights = (raised / jnp.sum(raised, axis=-1, keepdims=True)).astype(jnp.bfloat16)
    mixture = jnp.einsum(
        "ghps,gshd->gphd", weights, picked_values, preferred_element_type=jnp.float32
    )
    return mixture.astype(jnp.bfloat16)


def on_device(
    hidden, lengths, targets, attn_gain, w_query, w_key, w_value, w_out, final_gain, unembed
):
    phases = lax.axis_size("section")
    tensor_size = lax.axis_size("tensor")
    groups = lax.axis_size("dp")
    phase_at = lax.axis_index("section")
    tensor_at = lax.axis_index("tensor")
    group_at = lax.axis_index("dp")
    length = hidden.shape[1]
    model_width = hidden.shape[2]
    blocks = 4
    span_rows = length // blocks
    share_rows = span_rows // tensor_size
    gain_row = attn_gain[0]
    query_weight = w_query[0]
    key_weight = w_key[0]
    value_weight = w_value[0]
    out_weight = w_out[0]
    local_heads = query_weight.shape[1] // HD
    owners_all, places_all = segments(lengths, length)
    lead_dim = 1
    query_cols, output_rows = (
        lax.all_gather(query_weight, "dp", axis=1, tiled=True),
        lax.all_gather(out_weight, "dp", axis=0, tiled=True),
    )
    key_head = jnp.arange(groups * local_heads, dtype=jnp.int32) // (HEADS // KVH)
    key_owner = lax.dynamic_slice_in_dim(owners_all, group_at, 1, 0)
    key_place = lax.dynamic_slice_in_dim(places_all, group_at, 1, 0)

    def collect(normed):
        return lax.all_gather(normed, "tensor", axis=0, tiled=True)

    def arrange(flattened):
        return flattened.reshape(1, span_rows, flattened.shape[-1])

    def combine_heads(attended):
        flattened = attended.reshape(span_rows, attended.shape[-1])
        return lax.psum_scatter(
            jnp.dot(flattened, output_rows, preferred_element_type=jnp.float32),
            "tensor",
            scatter_dimension=0,
            tiled=True,
        )

    def layer(entering, item_at, active, key_cache, value_cache):
        normed = norm_round(entering, gain_row)
        gathered = collect(normed)
        queries = arrange(jnp.dot(gathered, query_cols, preferred_element_type=jnp.float32))
        key_rows = arrange(jnp.dot(gathered, key_weight, preferred_element_type=jnp.float32))
        value_rows = arrange(jnp.dot(gathered, value_weight, preferred_element_type=jnp.float32))
        block_start = item_at * span_rows
        block_places = lax.dynamic_slice_in_dim(key_place, block_start, span_rows, 1)
        block_owners = lax.dynamic_slice_in_dim(key_owner, block_start, span_rows, 1)
        queries = rotate(queries.reshape(lead_dim, span_rows, -1, HD), block_places).astype(
            jnp.bfloat16
        )
        key_rows = rotate(key_rows.reshape(lead_dim, span_rows, -1, HD), block_places).astype(
            jnp.bfloat16
        )
        value_rows = value_rows.reshape(lead_dim, span_rows, -1, HD).astype(jnp.bfloat16)
        key_cache = jnp.where(
            active, lax.dynamic_update_slice_in_dim(key_cache, key_rows, block_start, 1), key_cache
        )
        value_cache = jnp.where(
            active,
            lax.dynamic_update_slice_in_dim(value_cache, value_rows, block_start, 1),
            value_cache,
        )
        query_place = block_start + jnp.arange(span_rows, dtype=jnp.int32)
        attended = attend(
            queries, key_cache, value_cache, key_head, key_owner, block_owners, query_place
        )
        summed = combine_heads(attended.reshape(lead_dim, span_rows, -1))
        updated = (entering.astype(jnp.float32) + summed).astype(jnp.bfloat16)
        return (updated, key_cache, value_cache)

    def entry_rows(step_at):
        item_at = jnp.clip(step_at, 0, blocks - 1)
        return lax.dynamic_slice_in_dim(
            hidden[0], item_at * span_rows + tensor_at * share_rows, share_rows, 0
        )

    def store_final(finished, current, step_at):
        slot_at = step_at - phases
        storing = (phase_at == 0) & (slot_at >= 0) & (slot_at < blocks)
        placed = lax.dynamic_update_slice_in_dim(
            finished, current[None], jnp.clip(slot_at, 0, blocks - 1), 0
        )
        return jnp.where(storing, placed, finished)

    def advance(step_at, carried):
        current, key_cache, value_cache, finished = carried
        finished = store_final(finished, current, step_at)
        item_at = step_at - phase_at
        active = (item_at >= 0) & (item_at < blocks)
        entering = jnp.where(phase_at == 0, entry_rows(step_at), current)
        updated, key_cache, value_cache = layer(
            entering, jnp.clip(item_at, 0, blocks - 1), active, key_cache, value_cache
        )
        current = shifted(updated, "section", 1)
        return (current, key_cache, value_cache, finished)

    cache_shape = (lead_dim, length, key_weight.shape[1] // HD, HD)
    initial = (
        jnp.zeros((share_rows, model_width), jnp.bfloat16),
        jnp.zeros(cache_shape, jnp.bfloat16),
        jnp.zeros(cache_shape, jnp.bfloat16),
        jnp.zeros((blocks, share_rows, model_width), jnp.bfloat16),
    )
    carried = lax.fori_loop(0, blocks + phases - 1, advance, initial)
    finished = store_final(carried[3], carried[0], blocks + phases - 1)
    normed_final = norm_round(finished.reshape(blocks * share_rows, model_width), final_gain)
    shared = from_root(normed_final, "section", 0)
    every_row = lax.all_gather(shared, ("tensor", "dp"), axis=0, tiled=True)
    logits = jnp.dot(every_row, unembed, preferred_element_type=jnp.float32)
    vocab_cols = unembed.shape[1]
    target_order = (
        targets.reshape(groups, blocks, tensor_size, share_rows).transpose(2, 0, 1, 3).reshape(-1)
    )
    first_col = lax.axis_index(("section", "tensor", "dp")) * vocab_cols
    matches = target_order[:, None] == first_col + jnp.arange(vocab_cols, dtype=jnp.int32)[None, :]
    picked = jnp.sum(jnp.where(matches, logits, 0.0), axis=-1)
    highest = lax.pmax(jnp.max(logits, axis=-1), ("section", "tensor", "dp"))
    local_total = jnp.sum(jnp.exp(logits - highest[:, None]), axis=-1)
    summed_exp, chosen = lax.psum((local_total, picked), ("section", "tensor", "dp"))
    logprob = chosen - highest - jnp.log(summed_exp)
    return (
        logprob.reshape(tensor_size, groups, blocks, share_rows)
        .transpose(1, 2, 0, 3)
        .reshape(groups, length)
    )


def solution(mesh):
    in_specs = (
        P("dp", None, None),
        P(),
        P(),
        P("section", None),
        P("section", None, ("tensor", "dp")),
        P("section", None, "tensor"),
        P("section", None, "tensor"),
        P("section", ("tensor", "dp"), None),
        P(),
        P(None, ("section", "tensor", "dp")),
    )
    out_specs = P()
    return jax.shard_map(
        on_device, mesh=mesh, in_specs=in_specs, out_specs=out_specs, check_vma=False
    )
```

profile of v0, /device:TPU:0, one launch (start us, length us, event | category | flops | bytes accessed | tf_op | source)
XLA Modules:
  0.0 1721.7 jit_solution(11630918508003279162)
XLA Ops:
  8.3 564.7 %all-gather.8.cloned.1.call-done = bf16[1,8192,2048]{2,1,0:T(8,128)(2,1)} async-done(((bf16[1,8192,512]{2,1,0:T(8,128)(2,1)}), bf16[1,8192,2048]{2,1,0:T(8,128)(2,1)}) %all-gather.8.cloned.1.call-update) | async-done | bytes 33554448 | tf_op jit(solution)/shard_map/all_gather | solution.py:104
  573.1 561.2 %all-gather.10.cloned.1.call-done = bf16[1,2048,8192]{2,1,0:T(8,128)(2,1)} async-done(((bf16[1,512,8192]{2,1,0:T(8,128)(2,1)}), bf16[1,2048,8192]{2,1,0:T(8,128)(2,1)}) %all-gather.10.cloned.1.call-update) | async-done | bytes 33554448 | tf_op jit(solution)/shard_map/all_gather | solution.py:105
  1134.4 385.8 %while.23 = (s32[]{:T(128)}, bf16[8,8192]{1,0:T(8,128)(2,1)S(1)}, bf16[1,64,4,64]{3,1,2,0:T(8,128)(2,1)S(1)}, bf16[1,64,4,64]{3,1,2,0:T(8,128)(2,1)S(1)}, bf16[4...) while((s32[]{:T(128)}, bf16[8,8192]{1,0:T(8,128)(2,1)S(1)}, ...), condition=%wide.region_8.10_spmd.clone.clone, body=%wide.region_3.9_spmd.clone.clone.sunk | while | flops 1217971712 | bytes 85631256 | solution.py:191
  1143.7 12.8 fusion.106
  1160.1 13.6 fusion.113
  1173.8 6.3 reduce-scatter.2.cloned.1.call-done
  1182.9 4.9 collective-permute-done
  1197.0 12.8 fusion.106
  1213.4 13.6 fusion.113
  1227.1 8.3 reduce-scatter.2.cloned.1.call-done
  1238.3 4.9 collective-permute-done
  1252.4 12.8 fusion.106
  1268.9 13.6 fusion.113
  1282.5 8.3 reduce-scatter.2.cloned.1.call-done
  1293.7 4.9 collective-permute-done
  1307.8 12.8 fusion.106
  1324.3 13.6 fusion.113
  1337.9 8.3 reduce-scatter.2.cloned.1.call-done
  1363.2 12.8 fusion.106
  1379.7 13.6 fusion.113
  1393.3 8.4 reduce-scatter.2.cloned.1.call-done
  1418.6 12.8 fusion.106
  1435.1 13.6 fusion.113
  1448.8 8.4 reduce-scatter.2.cloned.1.call-done
  1474.0 12.8 fusion.106
  1490.5 13.6 fusion.113
  1504.2 8.4 reduce-scatter.2.cloned.1.call-done
  1521.9 47.5 %all-reduce.3.cloned.1.call-done = bf16[32,8192]{1,0:T(8,128)(2,1)} async-done(((bf16[32,8192]{1,0:T(8,128)(2,1)}), bf16[32,8192]{1,0:T(8,128)(2,1)}) %all-reduce.3.cloned.1.call-update) | async-done | bytes 524304 | tf_op jit(solution)/shard_map/psum | solution.py:24
  1569.6 48.5 %all-gather.6.cloned.1.call-done = bf16[256,8192]{1,0:T(8,128)(2,1)} async-done(((bf16[32,8192]{1,0:T(8,128)(2,1)}), bf16[256,8192]{1,0:T(8,128)(2,1)}) %all-gather.6.cloned.1.call-update) | async-done | bytes 4194320 | tf_op jit(solution)/shard_map/all_gather | solution.py:195
  1618.1 16.3 fusion.48
  1634.5 38.9 %pmax.7 = f32[256]{0:T(256)S(1)} all-reduce(f32[256]{0:T(256)S(1)} %get-tuple-element.521), channel_id=1, replica_groups=mesh['section'=4,'tensor'=2,'dp'=4] {'section','tensor','dp'}, use_global_device_ids=true, to_apply=%region_14.16 | all-reduce | flops 256 | bytes 2048 | tf_op jit(solution)/shard_map/pmax | solution.py:204
  1674.0 40.4 %all-reduce = (f32[256]{0:T(256)S(1)}, f32[256]{0:T(256)S(1)}) all-reduce(f32[256]{0:T(256)S(1)} %get-tuple-element.468, f32[256]{0:T(256)S(1)} %get-tuple-element.467), channel_id=1, replica_groups=mesh['section'=4,'tensor'=2,'dp'=4] {'section','tensor','dp'}, use_global_device_ids=true, to_apply=%region_16.18 | all-reduce | flops 512 | bytes 4096 | tf_op jit(solution)/shard_map/psum | solution.py:206
  (294 shorter events, 133.2 us)
Async XLA Ops:
  6.5 566.5 %all-gather.8.cloned.1.call-start = ((), (), s32[]{:S(2)}) async-start(), calls=%async_computation.3 | async-start | bytes 41943040 | tf_op jit(solution)/shard_map/all_gather | solution.py:104
  7.3 0.8 copy-start.2
  7.3 1127.1 %copy-start = (f32[1,8192]{1,0:T(1,128)S(1)}, f32[1,8192]{1,0:T(1,128)}, u32[]{:S(2)}) copy-start(f32[1,8192]{1,0:T(1,128)} %param.17) | copy-start | bytes 98308
  7.3 1127.0 %all-gather.10.cloned.1.call-start = ((), (), s32[]{:S(2)}) async-start(), calls=%async_computation.4 | async-start | bytes 41943040 | tf_op jit(solution)/shard_map/all_gather | solution.py:105
  1134.4 386.3 %copy-start.1 = (f32[8192]{0:T(1024)S(1)}, f32[8192]{0:T(1024)}, u32[]{:S(2)}) copy-start(f32[8192]{0:T(1024)} %param.22) | copy-start | bytes 98308
  1134.4 435.0 %copy-start.3 = (s32[4,64]{1,0:T(4,128)S(1)}, s32[4,64]{1,0:T(4,128)}, u32[]{:S(2)}) copy-start(s32[4,64]{1,0:T(4,128)} %param.16) | copy-start | bytes 3076
  1134.4 45.7 %reduce-scatter.2.cloned.1.call-start = ((), (), s32[]{:S(2)}) async-start(), calls=%async_computation.5 | async-start | bytes 786432 | tf_op jit(solution)/shard_map/while/body/eval_jaxpr/reduce_scatter | solution.py:119
  1181.0 6.7 collective-permute-start
  1187.7 47.7 %reduce-scatter.2.cloned.1.call-start = ((), (), s32[]{:S(2)}) async-start(), calls=%async_computation.5 | async-start | bytes 786432 | tf_op jit(solution)/shard_map/while/body/eval_jaxpr/reduce_scatter | solution.py:119
  1236.4 6.7 collective-permute-start
  1243.1 47.7 %reduce-scatter.2.cloned.1.call-start = ((), (), s32[]{:S(2)}) async-start(), calls=%async_computation.5 | async-start | bytes 786432 | tf_op jit(solution)/shard_map/while/body/eval_jaxpr/reduce_scatter | solution.py:119
  1291.9 6.7 collective-permute-start
  1298.5 47.7 %reduce-scatter.2.cloned.1.call-start = ((), (), s32[]{:S(2)}) async-start(), calls=%async_computation.5 | async-start | bytes 786432 | tf_op jit(solution)/shard_map/while/body/eval_jaxpr/reduce_scatter | solution.py:119
  1347.3 6.7 collective-permute-start
  1354.0 47.8 %reduce-scatter.2.cloned.1.call-start = ((), (), s32[]{:S(2)}) async-start(), calls=%async_computation.5 | async-start | bytes 786432 | tf_op jit(solution)/shard_map/while/body/eval_jaxpr/reduce_scatter | solution.py:119
  1402.7 6.6 collective-permute-start
  1409.4 47.8 %reduce-scatter.2.cloned.1.call-start = ((), (), s32[]{:S(2)}) async-start(), calls=%async_computation.5 | async-start | bytes 786432 | tf_op jit(solution)/shard_map/while/body/eval_jaxpr/reduce_scatter | solution.py:119
  1458.1 6.6 collective-permute-start
  1464.8 47.8 %reduce-scatter.2.cloned.1.call-start = ((), (), s32[]{:S(2)}) async-start(), calls=%async_computation.5 | async-start | bytes 786432 | tf_op jit(solution)/shard_map/while/body/eval_jaxpr/reduce_scatter | solution.py:119
  1513.5 6.6 collective-permute-start
  1520.2 49.2 %all-reduce.3.cloned.1.call-start = ((), (), s32[]{:S(2)}) async-start(), calls=%async_computation.1 | async-start | bytes 1048576 | tf_op jit(solution)/shard_map/psum | solution.py:24
  1521.7 96.5 %all-gather.6.cloned.1.call-start = ((), (), s32[]{:S(2)}) async-start(), calls=%async_computation.2 | async-start | bytes 4718592 | tf_op jit(solution)/shard_map/all_gather | solution.py:195
Sparse Core Ops, SparseCore 0:
  8.9 564.0 all-gather.7
  574.6 559.5 all-gather.9
  1173.9 6.1 reduce-scatter.1
  1227.2 8.1 reduce-scatter.1
  1282.6 8.1 reduce-scatter.1
  1338.0 8.1 reduce-scatter.1
  1393.5 8.2 reduce-scatter.1
  1448.9 8.2 reduce-scatter.1
  1504.3 8.2 reduce-scatter.1
  1523.7 45.5 all-reduce.2
  1571.0 47.1 all-gather.5
where the time goes:
time: 1720 us
  waiting for transfers between devices  1310 us (76%)
  matrix products  247 us (14%)
  blocking collectives  93.2 us (5%)
  other arithmetic  24.4 us (1%)
    all_gather x1, waiting for transfers between devices, on_device(): lax.all_gather(query_weight, 'dp', axis=1, tiled=True)  565 us
    all_gather x1, waiting for transfers between devices, on_device(): lax.all_gather(out_weight, 'dp', axis=0, tiled=True)  561 us
    dot_general x7, matrix products, combine_heads(): jnp.dot(flattened, output_rows, preferred_element_type=jnp.float32)  95.5 us
    dot_general x7, matrix products, layer(): jnp.dot(gathered, query_cols, preferred_element_type=jnp.float32)  89.7 us
    reduce_scatter x7, waiting for transfers between devices, combine_heads(): lax.psum_scatter(jnp.dot(flattened, output_rows, preferred_element_type=j...  56.4 us
    all_gather x1, waiting for transfers between devices, on_device(): every_row = lax.all_gather(shared, ('tensor', 'dp'), axis=0, tiled=True)  48.5 us
    psum x1, waiting for transfers between devices, from_root(): return lax.psum(jnp.where(mine, x, jnp.zeros_like(x)), axis)  47.5 us
    psum x1, blocking collectives, on_device(): lax.psum((local_total, picked), ('section', 'tensor', 'dp'))  40.4 us
  transfers between devices with their start and end apart: 18, of which 18 were waited for; matrix products, arithmetic and copies ran while one was open for 0% of the time, Pallas kernels for 0%

commit v1 on v0

--- a/solution.py
+++ b/solution.py
@@ -58,11 +58,9 @@
     )
 
 
-def attend(queries, key_rows, value_rows, key_head, key_owner, query_owner, query_place):
-    picked_keys = jnp.take(key_rows, key_head, axis=2)
-    picked_values = jnp.take(value_rows, key_head, axis=2)
+def attend(queries, key_rows, value_rows, key_owner, query_owner, query_place):
     scores = jnp.einsum(
-        "gphd,gshd->ghps", queries, picked_keys, preferred_element_type=jnp.float32
+        "gphd,gsd->ghps", queries, key_rows, preferred_element_type=jnp.float32
     ) * queries.shape[-1] ** (-0.5)
     key_place = jnp.arange(key_rows.shape[1], dtype=jnp.int32)
     allowed = (key_owner[:, None, :] == query_owner[:, :, None]) & (
@@ -73,7 +71,7 @@
     raised = jnp.where(allowed, jnp.exp(scores - highest), 0.0)
     weights = (raised / jnp.sum(raised, axis=-1, keepdims=True)).astype(jnp.bfloat16)
     mixture = jnp.einsum(
-        "ghps,gshd->gphd", weights, picked_values, preferred_element_type=jnp.float32
+        "ghps,gsd->gphd", weights, value_rows, preferred_element_type=jnp.float32
     )
     return mixture.astype(jnp.bfloat16)
 
@@ -99,46 +97,31 @@
     out_weight = w_out[0]
     local_heads = query_weight.shape[1] // HD
     owners_all, places_all = segments(lengths, length)
-    lead_dim = 1
-    query_cols, output_rows = (
-        lax.all_gather(query_weight, "dp", axis=1, tiled=True),
-        lax.all_gather(out_weight, "dp", axis=0, tiled=True),
-    )
-    key_head = jnp.arange(groups * local_heads, dtype=jnp.int32) // (HEADS // KVH)
-    key_owner = lax.dynamic_slice_in_dim(owners_all, group_at, 1, 0)
-    key_place = lax.dynamic_slice_in_dim(places_all, group_at, 1, 0)
-
-    def collect(normed):
-        return lax.all_gather(normed, "tensor", axis=0, tiled=True)
-
-    def arrange(flattened):
-        return flattened.reshape(1, span_rows, flattened.shape[-1])
-
-    def combine_heads(attended):
-        flattened = attended.reshape(span_rows, attended.shape[-1])
-        return lax.psum_scatter(
-            jnp.dot(flattened, output_rows, preferred_element_type=jnp.float32),
-            "tensor",
-            scatter_dimension=0,
-            tiled=True,
-        )
+    local_kv = key_weight.shape[1] // HD
+    first_head = (tensor_at * groups + group_at) * local_heads
+    kv_col = (first_head // (HEADS // KVH) - tensor_at * local_kv) * HD
+    kv_weight = jnp.concatenate(
+        [
+            lax.dynamic_slice_in_dim(key_weight, kv_col, HD, 1),
+            lax.dynamic_slice_in_dim(value_weight, kv_col, HD, 1),
+        ],
+        axis=1,
+    )
 
     def layer(entering, item_at, active, key_cache, value_cache):
         normed = norm_round(entering, gain_row)
-        gathered = collect(normed)
-        queries = arrange(jnp.dot(gathered, query_cols, preferred_element_type=jnp.float32))
-        key_rows = arrange(jnp.dot(gathered, key_weight, preferred_element_type=jnp.float32))
-        value_rows = arrange(jnp.dot(gathered, value_weight, preferred_element_type=jnp.float32))
+        gathered = lax.all_gather(normed, ("dp", "tensor"), axis=0, tiled=True)
+        queries = jnp.dot(gathered, query_weight, preferred_element_type=jnp.float32)
+        both = jnp.dot(gathered, kv_weight, preferred_element_type=jnp.float32)
         block_start = item_at * span_rows
-        block_places = lax.dynamic_slice_in_dim(key_place, block_start, span_rows, 1)
-        block_owners = lax.dynamic_slice_in_dim(key_owner, block_start, span_rows, 1)
-        queries = rotate(queries.reshape(lead_dim, span_rows, -1, HD), block_places).astype(
-            jnp.bfloat16
-        )
-        key_rows = rotate(key_rows.reshape(lead_dim, span_rows, -1, HD), block_places).astype(
-            jnp.bfloat16
-        )
-        value_rows = value_rows.reshape(lead_dim, span_rows, -1, HD).astype(jnp.bfloat16)
+        block_places = lax.dynamic_slice_in_dim(places_all, block_start, span_rows, 1)
+        block_owners = lax.dynamic_slice_in_dim(owners_all, block_start, span_rows, 1)
+        queries = rotate(
+            queries.reshape(groups, span_rows, local_heads, HD), block_places
+        ).astype(jnp.bfloat16)
+        key_rows = rotate(both[:, :HD].reshape(groups, span_rows, 1, HD), block_places)
+        key_rows = key_rows.reshape(groups, span_rows, HD).astype(jnp.bfloat16)
+        value_rows = both[:, HD:].reshape(groups, span_rows, HD).astype(jnp.bfloat16)
         key_cache = jnp.where(
             active, lax.dynamic_update_slice_in_dim(key_cache, key_rows, block_start, 1), key_cache
         )
@@ -149,9 +132,15 @@
         )
         query_place = block_start + jnp.arange(span_rows, dtype=jnp.int32)
         attended = attend(
-            queries, key_cache, value_cache, key_head, key_owner, block_owners, query_place
-        )
-        summed = combine_heads(attended.reshape(lead_dim, span_rows, -1))
+            queries, key_cache, value_cache, owners_all, block_owners, query_place
+        )
+        flattened = attended.reshape(groups * span_rows, local_heads * HD)
+        summed = lax.psum_scatter(
+            jnp.dot(flattened, out_weight, preferred_element_type=jnp.float32),
+            ("dp", "tensor"),
+            scatter_dimension=0,
+            tiled=True,
+        )
         updated = (entering.astype(jnp.float32) + summed).astype(jnp.bfloat16)
         return (updated, key_cache, value_cache)
 
@@ -181,7 +170,7 @@
         current = shifted(updated, "section", 1)
         return (current, key_cache, value_cache, finished)
 
-    cache_shape = (lead_dim, length, key_weight.shape[1] // HD, HD)
+    cache_shape = (groups, length, HD)
     initial = (
         jnp.zeros((share_rows, model_width), jnp.bfloat16),
         jnp.zeros(cache_shape, jnp.bfloat16),

time: 1720 us -> 808 us (0.47)
  waiting for transfers between devices: 1310 us -> 488 us
  matrix products: 247 us -> 120 us
  other arithmetic: 24.4 us -> 70.9 us
    all_gather x2 -> x7, waiting for transfers between devices: 1130 us -> 129 us  [layer(): gathered = lax.all_gather(normed, ('dp', 'tensor'), axis=0, tiled=True)]
    reduce_scatter x7, waiting for transfers between devices: 56.4 us -> 249 us  [layer(): lax.psum_scatter(jnp.dot(flattened, out_weight, preferred_element_type=jn...]
    dot_general x42 -> x35, matrix products: 230 us -> 104 us  [the longest x7 44.1 us: layer(): jnp.dot(flattened, out_weight, preferred_element_type=jnp.float32)]
  transfers between devices with their start and end apart: 18 -> 23, of which waited for: 18 -> 23; matrix products, arithmetic and copies ran while one was open for 0% -> 3% of each run, Pallas kernels for 0% -> 0%
where the time goes in v1:
time: 808 us; the launch traced here: 805 us
  waiting for transfers between devices  488 us (60%)
  matrix products  120 us (15%)
  blocking collectives  79.2 us (10%)
  other arithmetic  70.9 us (9%)
  local copies, waits for them, and re-layouts  19.8 us (2%)
  between operations  14.6 us (2%)
  starting transfers between devices  11.1 us (1%)
    reduce_scatter x7, waiting for transfers between devices, layer(): lax.psum_scatter(jnp.dot(flattened, out_weight, preferred_element_type=jn...  249 us
    all_gather x7, waiting for transfers between devices, layer(): gathered = lax.all_gather(normed, ('dp', 'tensor'), axis=0, tiled=True)  129 us
    all_gather x1, waiting for transfers between devices, on_device(): every_row = lax.all_gather(shared, ('tensor', 'dp'), axis=0, tiled=True)  48 us
    dot_general x7, matrix products, layer(): jnp.dot(flattened, out_weight, preferred_element_type=jnp.float32)  44.1 us
    psum x1, waiting for transfers between devices, from_root(): return lax.psum(jnp.where(mine, x, jnp.zeros_like(x)), axis)  42.1 us
    dot_general x7, matrix products, layer(): jnp.dot(gathered, query_weight, preferred_element_type=jnp.float32)  41.9 us
    psum x1, blocking collectives, on_device(): lax.psum((local_total, picked), ('section', 'tensor', 'dp'))  40.2 us
    pmax x1, blocking collectives, on_device(): highest = lax.pmax(jnp.max(logits, axis=-1), ('section', 'tensor', 'dp'))  39.1 us
  transfers between devices with their start and end apart: 23, of which 23 were waited for; matrix products, arithmetic and copies ran while one was open for 3% of the time, Pallas kernels for 0%

profile of v1, /device:TPU:0, one launch (start us, length us, event | category | flops | bytes accessed | tf_op | source)
XLA Modules:
  0.0 805.2 jit_solution(7202346753354979841)
XLA Ops:
  16.2 589.4 %while.21 = (s32[]{:T(128)}, bf16[8,8192]{1,0:T(8,128)(2,1)S(1)}, bf16[4,64,64]{2,1,0:T(8,128)(2,1)}, bf16[4,64,64]{2,1,0:T(8,128)(2,1)}, bf16[4,8,8192]{2,1,0:T...) while((s32[]{:T(128)}, bf16[8,8192]{1,0:T(8,128)(2,1)S(1)}, ...), condition=%wide.region_8.9_spmd, body=%wide.region_3.8_spmd.sunk | while | flops 1217812224 | bytes 43662532 | solution.py:180
  20.8 23.0 %all-gather.5.cloned.1.call-done = bf16[64,8192]{1,0:T(8,128)(2,1)} async-done(((bf16[8,8192]{1,0:T(8,128)(2,1)}), bf16[64,8192]{1,0:T(8,128)(2,1)}) %all-gather.5.cloned.1.call-update) | async-done | bytes 1048592 | tf_op jit(solution)/shard_map/while/body/eval_jaxpr/all_gather | solution.py:113
  43.9 6.0 fusion.97
  56.2 6.3 fusion.106
  62.6 35.7 %reduce-scatter.2.cloned.1.call-done = f32[8,8192]{1,0:T(8,128)} async-done(((f32[64,8192]{1,0:T(8,128)}), f32[8,8192]{1,0:T(8,128)}) %reduce-scatter.2.cloned.1.call-update) | async-done | bytes 262160 | tf_op jit(solution)/shard_map/while/body/eval_jaxpr/reduce_scatter | solution.py:138
  109.8 17.5 %all-gather.5.cloned.1.call-done = bf16[64,8192]{1,0:T(8,128)(2,1)} async-done(((bf16[8,8192]{1,0:T(8,128)(2,1)}), bf16[64,8192]{1,0:T(8,128)(2,1)}) %all-gather.5.cloned.1.call-update) | async-done | bytes 1048592 | tf_op jit(solution)/shard_map/while/body/eval_jaxpr/all_gather | solution.py:113
  127.3 6.0 fusion.97
  139.6 6.3 fusion.106
  146.0 35.6 %reduce-scatter.2.cloned.1.call-done = f32[8,8192]{1,0:T(8,128)} async-done(((f32[64,8192]{1,0:T(8,128)}), f32[8,8192]{1,0:T(8,128)}) %reduce-scatter.2.cloned.1.call-update) | async-done | bytes 262160 | tf_op jit(solution)/shard_map/while/body/eval_jaxpr/reduce_scatter | solution.py:138
  193.1 17.6 %all-gather.5.cloned.1.call-done = bf16[64,8192]{1,0:T(8,128)(2,1)} async-done(((bf16[8,8192]{1,0:T(8,128)(2,1)}), bf16[64,8192]{1,0:T(8,128)(2,1)}) %all-gather.5.cloned.1.call-update) | async-done | bytes 1048592 | tf_op jit(solution)/shard_map/while/body/eval_jaxpr/all_gather | solution.py:113
  210.7 6.0 fusion.97
  223.0 6.3 fusion.106
  229.4 35.5 %reduce-scatter.2.cloned.1.call-done = f32[8,8192]{1,0:T(8,128)} async-done(((f32[64,8192]{1,0:T(8,128)}), f32[8,8192]{1,0:T(8,128)}) %reduce-scatter.2.cloned.1.call-update) | async-done | bytes 262160 | tf_op jit(solution)/shard_map/while/body/eval_jaxpr/reduce_scatter | solution.py:138
  276.4 17.7 %all-gather.5.cloned.1.call-done = bf16[64,8192]{1,0:T(8,128)(2,1)} async-done(((bf16[8,8192]{1,0:T(8,128)(2,1)}), bf16[64,8192]{1,0:T(8,128)(2,1)}) %all-gather.5.cloned.1.call-update) | async-done | bytes 1048592 | tf_op jit(solution)/shard_map/while/body/eval_jaxpr/all_gather | solution.py:113
  294.1 6.0 fusion.97
  306.5 6.3 fusion.106
  312.8 35.6 %reduce-scatter.2.cloned.1.call-done = f32[8,8192]{1,0:T(8,128)} async-done(((f32[64,8192]{1,0:T(8,128)}), f32[8,8192]{1,0:T(8,128)}) %reduce-scatter.2.cloned.1.call-update) | async-done | bytes 262160 | tf_op jit(solution)/shard_map/while/body/eval_jaxpr/reduce_scatter | solution.py:138
  360.0 17.6 %all-gather.5.cloned.1.call-done = bf16[64,8192]{1,0:T(8,128)(2,1)} async-done(((bf16[8,8192]{1,0:T(8,128)(2,1)}), bf16[64,8192]{1,0:T(8,128)(2,1)}) %all-gather.5.cloned.1.call-update) | async-done | bytes 1048592 | tf_op jit(solution)/shard_map/while/body/eval_jaxpr/all_gather | solution.py:113
  377.6 6.0 fusion.97
  389.9 6.3 fusion.106
  396.3 35.6 %reduce-scatter.2.cloned.1.call-done = f32[8,8192]{1,0:T(8,128)} async-done(((f32[64,8192]{1,0:T(8,128)}), f32[8,8192]{1,0:T(8,128)}) %reduce-scatter.2.cloned.1.call-update) | async-done | bytes 262160 | tf_op jit(solution)/shard_map/while/body/eval_jaxpr/reduce_scatter | solution.py:138
  443.4 17.6 %all-gather.5.cloned.1.call-done = bf16[64,8192]{1,0:T(8,128)(2,1)} async-done(((bf16[8,8192]{1,0:T(8,128)(2,1)}), bf16[64,8192]{1,0:T(8,128)(2,1)}) %all-gather.5.cloned.1.call-update) | async-done | bytes 1048592 | tf_op jit(solution)/shard_map/while/body/eval_jaxpr/all_gather | solution.py:113
  473.3 6.3 fusion.106
  479.7 35.6 %reduce-scatter.2.cloned.1.call-done = f32[8,8192]{1,0:T(8,128)} async-done(((f32[64,8192]{1,0:T(8,128)}), f32[8,8192]{1,0:T(8,128)}) %reduce-scatter.2.cloned.1.call-update) | async-done | bytes 262160 | tf_op jit(solution)/shard_map/while/body/eval_jaxpr/reduce_scatter | solution.py:138
  526.8 17.6 %all-gather.5.cloned.1.call-done = bf16[64,8192]{1,0:T(8,128)(2,1)} async-done(((bf16[8,8192]{1,0:T(8,128)(2,1)}), bf16[64,8192]{1,0:T(8,128)(2,1)}) %all-gather.5.cloned.1.call-update) | async-done | bytes 1048592 | tf_op jit(solution)/shard_map/while/body/eval_jaxpr/all_gather | solution.py:113
  556.8 6.3 fusion.106
  563.1 35.6 %reduce-scatter.2.cloned.1.call-done = f32[8,8192]{1,0:T(8,128)} async-done(((f32[64,8192]{1,0:T(8,128)}), f32[8,8192]{1,0:T(8,128)}) %reduce-scatter.2.cloned.1.call-update) | async-done | bytes 262160 | tf_op jit(solution)/shard_map/while/body/eval_jaxpr/reduce_scatter | solution.py:138
  610.8 42.1 %all-reduce.3.cloned.1.call-done = bf16[32,8192]{1,0:T(8,128)(2,1)} async-done(((bf16[32,8192]{1,0:T(8,128)(2,1)}), bf16[32,8192]{1,0:T(8,128)(2,1)}) %all-reduce.3.cloned.1.call-update) | async-done | bytes 524304 | tf_op jit(solution)/shard_map/psum | solution.py:24
  653.1 48.0 %all-gather.3.cloned.1.call-done = bf16[256,8192]{1,0:T(8,128)(2,1)} async-done(((bf16[32,8192]{1,0:T(8,128)(2,1)}), bf16[256,8192]{1,0:T(8,128)(2,1)}) %all-gather.3.cloned.1.call-update) | async-done | bytes 4194320 | tf_op jit(solution)/shard_map/all_gather | solution.py:184
  701.1 16.3 %fusion.49 = (f32[256]{0:T(256)S(1)}, f32[256,2048]{1,0:T(8,128)S(1)}) fusion(bf16[256,8192]{1,0:T(8,128)(2,1)} %all-gather.3.cloned.1.call-done, bf16[8192,2048]{1,0:T(8,128)(2,1)} %param.21), kind=kOutput, calls=%fused_computation.85 | convolution fusion | flops 8590458880 | bytes 39846912 | tf_op jit(solution)/shard_map/dot_general | solution.py:185
  717.4 39.1 %pmax.7 = f32[256]{0:T(256)S(1)} all-reduce(f32[256]{0:T(256)S(1)} %get-tuple-element.395), channel_id=1, replica_groups=mesh['section'=4,'tensor'=2,'dp'=4] {'section','tensor','dp'}, use_global_device_ids=true, to_apply=%region_14.15 | all-reduce | flops 256 | bytes 2048 | tf_op jit(solution)/shard_map/pmax | solution.py:193
  757.1 40.2 %all-reduce = (f32[256]{0:T(256)S(1)}, f32[256]{0:T(256)S(1)}) all-reduce(f32[256]{0:T(256)S(1)} %get-tuple-element.348, f32[256]{0:T(256)S(1)} %get-tuple-element.347), channel_id=1, replica_groups=mesh['section'=4,'tensor'=2,'dp'=4] {'section','tensor','dp'}, use_global_device_ids=true, to_apply=%region_16.17 | all-reduce | flops 512 | bytes 4096 | tf_op jit(solution)/shard_map/psum | solution.py:195
  (374 shorter events, 151.4 us)
Async XLA Ops:
  16.2 27.6 %copy-start.1 = (bf16[8,8192]{1,0:T(8,128)(2,1)}, bf16[8,8192]{1,0:T(8,128)(2,1)S(1)}, u32[]{:S(2)}) copy-start(bf16[8,8192]{1,0:T(8,128)(2,1)S(1)} %get-tuple-element.537) | copy-start | bytes 393220 | tf_op jit(solution)/shard_map/while
  16.2 27.6 %all-gather.5.cloned.1.call-start = ((), (), s32[]{:S(2)}) async-start(), calls=%async_computation.3 | async-start | bytes 1179648 | tf_op jit(solution)/shard_map/while/body/eval_jaxpr/all_gather | solution.py:113
  18.9 79.3 %reduce-scatter.2.cloned.1.call-start = ((), (), s32[]{:S(2)}) async-start(), calls=%async_computation.4 | async-start | bytes 2359296 | tf_op jit(solution)/shard_map/while/body/eval_jaxpr/reduce_scatter | solution.py:138
  62.5 38.1 %copy-start.2 = (bf16[8,8192]{1,0:T(8,128)(2,1)S(1)}, bf16[8,8192]{1,0:T(8,128)(2,1)}, u32[]{:S(2)}) copy-start(bf16[8,8192]{1,0:T(8,128)(2,1)} %copy-done.1) | copy-start | bytes 393220 | tf_op jit(solution)/shard_map/while
  99.2 5.9 collective-permute-start
  105.2 22.1 %all-gather.5.cloned.1.call-start = ((), (), s32[]{:S(2)}) async-start(), calls=%async_computation.3 | async-start | bytes 1179648 | tf_op jit(solution)/shard_map/while/body/eval_jaxpr/all_gather | solution.py:113
  107.9 73.7 %reduce-scatter.2.cloned.1.call-start = ((), (), s32[]{:S(2)}) async-start(), calls=%async_computation.4 | async-start | bytes 2359296 | tf_op jit(solution)/shard_map/while/body/eval_jaxpr/reduce_scatter | solution.py:138
  145.9 38.1 %copy-start.2 = (bf16[8,8192]{1,0:T(8,128)(2,1)S(1)}, bf16[8,8192]{1,0:T(8,128)(2,1)}, u32[]{:S(2)}) copy-start(bf16[8,8192]{1,0:T(8,128)(2,1)} %copy-done.1) | copy-start | bytes 393220 | tf_op jit(solution)/shard_map/while
  182.5 5.9 collective-permute-start
  188.5 22.2 %all-gather.5.cloned.1.call-start = ((), (), s32[]{:S(2)}) async-start(), calls=%async_computation.3 | async-start | bytes 1179648 | tf_op jit(solution)/shard_map/while/body/eval_jaxpr/all_gather | solution.py:113
  191.2 73.7 %reduce-scatter.2.cloned.1.call-start = ((), (), s32[]{:S(2)}) async-start(), calls=%async_computation.4 | async-start | bytes 2359296 | tf_op jit(solution)/shard_map/while/body/eval_jaxpr/reduce_scatter | solution.py:138
  229.3 38.1 %copy-start.2 = (bf16[8,8192]{1,0:T(8,128)(2,1)S(1)}, bf16[8,8192]{1,0:T(8,128)(2,1)}, u32[]{:S(2)}) copy-start(bf16[8,8192]{1,0:T(8,128)(2,1)} %copy-done.1) | copy-start | bytes 393220 | tf_op jit(solution)/shard_map/while
  265.9 5.9 collective-permute-start
  271.8 22.3 %all-gather.5.cloned.1.call-start = ((), (), s32[]{:S(2)}) async-start(), calls=%async_computation.3 | async-start | bytes 1179648 | tf_op jit(solution)/shard_map/while/body/eval_jaxpr/all_gather | solution.py:113
  274.5 73.9 %reduce-scatter.2.cloned.1.call-start = ((), (), s32[]{:S(2)}) async-start(), calls=%async_computation.4 | async-start | bytes 2359296 | tf_op jit(solution)/shard_map/while/body/eval_jaxpr/reduce_scatter | solution.py:138
  312.8 38.1 %copy-start.2 = (bf16[8,8192]{1,0:T(8,128)(2,1)S(1)}, bf16[8,8192]{1,0:T(8,128)(2,1)}, u32[]{:S(2)}) copy-start(bf16[8,8192]{1,0:T(8,128)(2,1)} %copy-done.1) | copy-start | bytes 393220 | tf_op jit(solution)/shard_map/while
  349.4 5.9 collective-permute-start
  355.4 22.2 %all-gather.5.cloned.1.call-start = ((), (), s32[]{:S(2)}) async-start(), calls=%async_computation.3 | async-start | bytes 1179648 | tf_op jit(solution)/shard_map/while/body/eval_jaxpr/all_gather | solution.py:113
  358.1 73.8 %reduce-scatter.2.cloned.1.call-start = ((), (), s32[]{:S(2)}) async-start(), calls=%async_computation.4 | async-start | bytes 2359296 | tf_op jit(solution)/shard_map/while/body/eval_jaxpr/reduce_scatter | solution.py:138
  396.2 38.1 %copy-start.2 = (bf16[8,8192]{1,0:T(8,128)(2,1)S(1)}, bf16[8,8192]{1,0:T(8,128)(2,1)}, u32[]{:S(2)}) copy-start(bf16[8,8192]{1,0:T(8,128)(2,1)} %copy-done.1) | copy-start | bytes 393220 | tf_op jit(solution)/shard_map/while
  432.8 5.9 collective-permute-start
  438.8 22.2 %all-gather.5.cloned.1.call-start = ((), (), s32[]{:S(2)}) async-start(), calls=%async_computation.3 | async-start | bytes 1179648 | tf_op jit(solution)/shard_map/while/body/eval_jaxpr/all_gather | solution.py:113
  441.5 73.8 %reduce-scatter.2.cloned.1.call-start = ((), (), s32[]{:S(2)}) async-start(), calls=%async_computation.4 | async-start | bytes 2359296 | tf_op jit(solution)/shard_map/while/body/eval_jaxpr/reduce_scatter | solution.py:138
  479.6 38.1 %copy-start.2 = (bf16[8,8192]{1,0:T(8,128)(2,1)S(1)}, bf16[8,8192]{1,0:T(8,128)(2,1)}, u32[]{:S(2)}) copy-start(bf16[8,8192]{1,0:T(8,128)(2,1)} %copy-done.1) | copy-start | bytes 393220 | tf_op jit(solution)/shard_map/while
  516.2 5.9 collective-permute-start
  522.2 22.2 %all-gather.5.cloned.1.call-start = ((), (), s32[]{:S(2)}) async-start(), calls=%async_computation.3 | async-start | bytes 1179648 | tf_op jit(solution)/shard_map/while/body/eval_jaxpr/all_gather | solution.py:113
  524.9 73.8 %reduce-scatter.2.cloned.1.call-start = ((), (), s32[]{:S(2)}) async-start(), calls=%async_computation.4 | async-start | bytes 2359296 | tf_op jit(solution)/shard_map/while/body/eval_jaxpr/reduce_scatter | solution.py:138
  563.1 38.1 %copy-start.2 = (bf16[8,8192]{1,0:T(8,128)(2,1)S(1)}, bf16[8,8192]{1,0:T(8,128)(2,1)}, u32[]{:S(2)}) copy-start(bf16[8,8192]{1,0:T(8,128)(2,1)} %copy-done.1) | copy-start | bytes 393220 | tf_op jit(solution)/shard_map/while
  599.7 5.9 collective-permute-start
  605.6 47.3 %copy-start.9 = (s32[4,64]{1,0:T(4,128)S(1)}, s32[4,64]{1,0:T(4,128)}, u32[]{:S(2)}) copy-start(s32[4,64]{1,0:T(4,128)} %param.14) | copy-start | bytes 3076
  605.6 47.2 %all-reduce.3.cloned.1.call-start = ((), (), s32[]{:S(2)}) async-start(), calls=%async_computation.1 | async-start | bytes 1048576 | tf_op jit(solution)/shard_map/psum | solution.py:24
  610.7 90.4 %all-gather.3.cloned.1.call-start = ((), (), s32[]{:S(2)}) async-start(), calls=%async_computation.2 | async-start | bytes 4718592 | tf_op jit(solution)/shard_map/all_gather | solution.py:184
  (55 other events, 354.6 us)
Sparse Core Ops, SparseCore 0:
  19.0 24.7 all-gather.4
  62.7 35.5 reduce-scatter.1
  108.0 19.2 all-gather.4
  146.1 35.4 reduce-scatter.1
  191.3 19.3 all-gather.4
  229.5 35.3 reduce-scatter.1
  274.6 19.4 all-gather.4
  312.9 35.4 reduce-scatter.1
  358.2 19.3 all-gather.4
  396.4 35.4 reduce-scatter.1
  441.6 19.3 all-gather.4
  479.8 35.4 reduce-scatter.1
  525.0 19.3 all-gather.4
  563.2 35.4 reduce-scatter.1
Sparse Core Ops, SparseCore 1:
  610.8 42.0 all-reduce.2
  654.3 46.7 all-gather.2
